TPU v7x, 256 devices: a whole 4x4x8 slice. The times are simulated.
256 devices in a mesh: replica: 16 (over z, core), mp: 16 (over y, x).
Axes of the slice: x: 4, y: 4, z: 8, core: 2. Of those that a mesh axis runs over, the one named last changes fastest.
Arguments:
- pre_act: bfloat16 [2400, 32768], P('mp', 'replica'), may hold values from -6 to 6
- out_grad: bfloat16 [32768, 4800], P(('replica', 'mp')), may hold values from -6 to 6
- weight: bfloat16 [2400, 4800], P('mp'), may hold values from -0.09375 to 0.09375
- error: float32 [16, 2400, 4800], P('replica', 'mp'), may hold values from -96 to 96
- q_init: float32 [4800, 32], replicated, may hold values from -6 to 6
Outputs:
- pre_grad: bfloat16 [2400, 32768], P('mp', 'replica')
- new_error: float32 [16, 2400, 4800], P('replica', 'mp')
- q_new: float32 [4800, 32], replicated
All inputs are finite; a program needn't handle non-finite values.
Results may differ from a plain program's by a relative error of at most 0.013.
Values may be sent and summed in bfloat16 or wider, within the bound.
No kernel may reach another device: no remote copies, remote signals or barrier semaphores. Data moves between devices by JAX's collectives and lax.ppermute only.
A program may use at most 128 MiB of HBM per device.

v0:
```python
import jax
import jax.numpy as jnp
from jax import lax
from jax.sharding import PartitionSpec as P


def gelu_back(pre, grad):
    _, pull = jax.vjp(jax.nn.gelu, pre)
    return pull(grad)[0]


def shards(pre_act, out_grad, weight, error, q_init):
    hi = lax.Precision.HIGHEST
    groups = lax.axis_size("replica")
    act = jax.nn.gelu(pre_act.astype(jnp.float32)).astype(jnp.bfloat16)
    piece = lax.all_gather(out_grad, "mp", axis=0, tiled=True)
    back = jnp.einsum("kf,hf->hk", piece, weight, preferred_element_type=jnp.float32)
    pre_slice = pre_act.astype(jnp.float32)
    update = gelu_back(pre_slice, back).astype(jnp.bfloat16)
    pre_grad = update
    grad = jnp.dot(act, piece, preferred_element_type=jnp.float32)
    grad, pre_grad = (grad, pre_grad)
    mat = grad + error[0]
    p_local = jnp.dot(mat, q_init, precision=hi)
    pbar = lax.psum(p_local, "replica") / groups
    gram = lax.psum(jnp.dot(pbar.T, pbar, precision=hi), "mp")
    lower = jnp.linalg.cholesky(gram)
    phat = jax.scipy.linalg.solve_triangular(lower, pbar.T, lower=True).T
    q_local = jnp.dot(mat.T, phat, precision=hi)
    q_new = lax.psum(q_local, ("replica", "mp")) / groups
    approx = jnp.dot(phat, q_new.T, precision=hi)
    new_error = (mat - approx)[None]
    return (pre_grad, new_error, q_new)


def solution(mesh):
    return jax.shard_map(
        shards,
        mesh=mesh,
        in_specs=(
            P("mp", "replica"),
            P(("replica", "mp"), None),
            P("mp", None),
            P("replica", "mp", None),
            P(),
        ),
        out_specs=(P("mp", "replica"), P("replica", "mp", None), P()),
        check_vma=False,
    )
```

profile of v0, /device:TPU:2, one launch (start us, length us, event | category | flops | bytes accessed | tf_op | source)
XLA Modules:
  0.0 564.8 jit_solution(16882801023573134399)
XLA Ops:
  7.2 0.0 copy-start
  7.2 0.0 all-gather.2.cloned.1.call-start
  7.2 0.7 all-gather.2.cloned.1.call-update
  7.9 0.0 copy-start.3
  7.9 0.0 all-reduce.2.cloned.1.call-start
  8.0 145.9 %all-gather.2.cloned.1.call-done = bf16[2048,4800]{0,1:T(8,128)(2,1)} async-done(((bf16[128,4800]{0,1:T(8,128)(2,1)}), bf16[2048,4800]{0,1:T(8,128)(2,1)}) %all-gather.2.cloned.1.call-update) | async-done | bytes 19660816 | tf_op jit(solution)/shard_map/all_gather | solution.py:16
  153.8 11.3 %convolution_add_fusion = f32[150,4800]{1,0:T(8,128)S(1)} fusion(bf16[2048,4800]{0,1:T(8,128)(2,1)} %all-gather.2.cloned.1.call-done, f32[1,150,4800]{2,0,1:T(1,128)} %param.8, bf16[150,2048]{1,0:T(8,128)(2,1)} %param.5), kind=kOutput, calls=%fused_computation.2 | convolution fusion | flops 2952911872 | bytes 26035200 | tf_op jit(solution)/shard_map/dot_general | solution.py:21
  165.2 0.0 copy-start.1
  165.2 1.6 copy-done.1
  166.8 0.0 copy-done.3
  166.8 2.8 fusion.31
  169.6 47.5 %psum.21 = f32[150,32]{0,1:T(8,128)S(1)} all-reduce(f32[150,32]{0,1:T(8,128)S(1)} %fusion.31), channel_id=1, replica_groups=mesh['replica'=16,'mp'=16] {'replica'}, use_global_device_ids=true, to_apply=%region_0.0 | all-reduce | flops 4800 | bytes 38400 | tf_op jit(solution)/shard_map/psum | solution.py:25
  217.1 0.2 fusion.18
  217.3 67.4 %psum.22 = f32[32,32]{0,1:T(8,128)S(1)} all-reduce(f32[32,32]{0,1:T(8,128)S(1)} %fusion.18), channel_id=1, replica_groups=mesh['replica'=16,'mp'=16] {'mp'}, use_global_device_ids=true, to_apply=%region_1.0 | all-reduce | flops 1024 | bytes 8192 | tf_op jit(solution)/shard_map/psum | solution.py:26
  284.6 0.1 copy.9
  284.7 2.9 cholesky.16
  287.6 0.6 compare_reduce_fusion
  288.3 0.7 fusion.20
  288.9 2.4 custom-call.7
  291.4 0.2 fusion.16
  291.6 0.0 copy-start.4
  291.6 4.7 fusion.32
  296.4 0.0 all-reduce.2.cloned.1.call-update
  296.4 0.0 copy-done
  296.4 0.0 copy-done.4
  296.4 11.3 %fusion.4 = bf16[150,2048]{1,0:T(8,128)(2,1)} fusion(bf16[150,2048]{1,0:T(8,128)(2,1)S(1)} %copy-done.4, bf16[150,4800]{1,0:T(8,128)(2,1)S(1)} %copy-done, bf16[2048,4800]{0,1:T(8,128)(2,1)} %all-gather.2.cloned.1.call-done), kind=kOutput, calls=%fused_computation.11 | convolution fusion | flops 2955571200 | bytes 22329600 | tf_op jit(solution)/shard_map/kf,hf->hk/dot_general | solution.py:17
  307.8 239.8 %all-reduce.2.cloned.1.call-done = f32[4800,32]{0,1:T(8,128)} async-done(((f32[4800,32]{0,1:T(8,128)}), f32[4800,32]{0,1:T(8,128)}) %all-reduce.2.cloned.1.call-update) | async-done | bytes 614416 | tf_op jit(solution)/shard_map/psum | solution.py:30
  547.6 1.1 broadcast_multiply_fusion
  548.7 0.0 copy-start.2
  548.7 4.6 fusion
  553.3 0.0 copy-done.2
  553.3 4.6 copy.10
  (2 shorter events, 0.0 us)
Async XLA Ops:
  7.2 289.3 %copy-start = (bf16[150,4800]{1,0:T(8,128)(2,1)S(1)}, bf16[150,4800]{1,0:T(8,128)(2,1)}, u32[]{:S(2)}) copy-start(bf16[150,4800]{1,0:T(8,128)(2,1)} %param.7) | copy-start | bytes 4320004
  7.2 146.7 %all-gather.2.cloned.1.call-start = ((), (), s32[]{:S(2)}) async-start(), calls=%async_computation | async-start | bytes 20889600 | tf_op jit(solution)/shard_map/all_gather | solution.py:16
  7.9 158.9 %copy-start.3 = (f32[4800,32]{0,1:T(8,128)S(1)}, f32[4800,32]{0,1:T(8,128)}, u32[]{:S(2)}) copy-start(f32[4800,32]{0,1:T(8,128)} %param.9) | copy-start | bytes 1843204
  7.9 539.6 %all-reduce.2.cloned.1.call-start = ((), (), s32[]{:S(2)}) async-start(), calls=%async_computation.1 | async-start | bytes 1245184 | tf_op jit(solution)/shard_map/psum | solution.py:30
  165.2 1.7 copy-start.1
  291.6 4.8 copy-start.4
  548.7 4.7 copy-start.2
Sparse Core Ops, SparseCore 0:
  10.4 143.3 all-gather.1
  296.5 250.9 all-reduce.1
where the time goes:
time: 565 us
  waiting for transfers between devices  386 us (68%)
  blocking collectives  115 us (20%)
  matrix products  35.2 us (6%)
  between operations  14.2 us (3%)
  other arithmetic  7.8 us (1%)
  local copies, waits for them, and re-layouts  6.33 us (1%)
    psum x1, waiting for transfers between devices, shards(): q_new = lax.psum(q_local, ('replica', 'mp')) / groups  240 us
    all_gather x1, waiting for transfers between devices, shards(): piece = lax.all_gather(out_grad, 'mp', axis=0, tiled=True)  146 us
    psum x1, blocking collectives, shards(): gram = lax.psum(jnp.dot(pbar.T, pbar, precision=hi), 'mp')  67.4 us
    psum x1, blocking collectives, shards(): pbar = lax.psum(p_local, 'replica') / groups  47.5 us
    dot_general x1, matrix products, shards(): grad = jnp.dot(act, piece, preferred_element_type=jnp.float32)  11.3 us
    dot_general x1, matrix products, shards(): jnp.einsum('kf,hf->hk', piece, weight, preferred_element_type=jnp.float32)  11.3 us
  transfers between devices with their start and end apart: 2, of which 2 were waited for; matrix products, arithmetic and copies ran while one was open for 2% of the time, Pallas kernels for 0%

commit v1 on v0

--- a/solution.py
+++ b/solution.py
@@ -27,7 +27,7 @@
     lower = jnp.linalg.cholesky(gram)
     phat = jax.scipy.linalg.solve_triangular(lower, pbar.T, lower=True).T
     q_local = jnp.dot(mat.T, phat, precision=hi)
-    q_new = lax.psum(q_local, ("replica", "mp")) / groups
+    q_new = lax.psum(lax.psum(q_local, "replica"), "mp") / groups
     approx = jnp.dot(phat, q_new.T, precision=hi)
     new_error = (mat - approx)[None]
     return (pre_grad, new_error, q_new)

time: 565 us -> 523 us (0.926)
  waiting for transfers between devices: 386 us -> 344 us
    psum x1 -> x2, waiting for transfers between devices: 240 us -> 197 us  [shards(): q_new = lax.psum(lax.psum(q_local, 'replica'), 'mp') / groups]
  transfers between devices with their start and end apart: 2 -> 3, of which waited for: 2 -> 3; matrix products, arithmetic and copies ran while one was open for 2% -> 2% of each run, Pallas kernels for 0% -> 0%
where the time goes in v1:
time: 523 us; the launch traced here: 522 us
  waiting for transfers between devices  344 us (66%)
  blocking collectives  115 us (22%)
  matrix products  35.2 us (7%)
  between operations  13.9 us (3%)
  other arithmetic  7.8 us (1%)
  local copies, waits for them, and re-layouts  6.33 us (1%)
    psum x2, waiting for transfers between devices, shards(): q_new = lax.psum(lax.psum(q_local, 'replica'), 'mp') / groups  197 us
    all_gather x1, waiting for transfers between devices, shards(): piece = lax.all_gather(out_grad, 'mp', axis=0, tiled=True)  146 us
    psum x1, blocking collectives, shards(): gram = lax.psum(jnp.dot(pbar.T, pbar, precision=hi), 'mp')  67.4 us
    psum x1, blocking collectives, shards(): pbar = lax.psum(p_local, 'replica') / groups  47.5 us
    dot_general x1, matrix products, shards(): grad = jnp.dot(act, piece, preferred_element_type=jnp.float32)  11.3 us
    dot_general x1, matrix products, shards(): jnp.einsum('kf,hf->hk', piece, weight, preferred_element_type=jnp.float32)  11.3 us
  transfers between devices with their start and end apart: 3, of which 3 were waited for; matrix products, arithmetic and copies ran while one was open for 2% of the time, Pallas kernels for 0%

profile of v1, /device:TPU:2, one launch (start us, length us, event | category | flops | bytes accessed | tf_op | source)
XLA Modules:
  0.0 522.1 jit_solution(11698353156846390881)
XLA Ops:
  7.2 0.0 copy-start
  7.2 0.0 all-gather.2.cloned.1.call-start
  7.2 0.7 all-gather.2.cloned.1.call-update
  7.9 0.0 copy-start.3
  7.9 0.0 all-reduce.3.cloned.1.call-start
  8.0 145.9 %all-gather.2.cloned.1.call-done = bf16[2048,4800]{0,1:T(8,128)(2,1)} async-done(((bf16[128,4800]{0,1:T(8,128)(2,1)}), bf16[2048,4800]{0,1:T(8,128)(2,1)}) %all-gather.2.cloned.1.call-update) | async-done | bytes 19660816 | tf_op jit(solution)/shard_map/all_gather | solution.py:16
  153.8 11.3 %convolution_add_fusion = f32[150,4800]{1,0:T(8,128)S(1)} fusion(bf16[2048,4800]{0,1:T(8,128)(2,1)} %all-gather.2.cloned.1.call-done, f32[1,150,4800]{2,0,1:T(1,128)} %param.8, bf16[150,2048]{1,0:T(8,128)(2,1)} %param.5), kind=kOutput, calls=%fused_computation.2 | convolution fusion | flops 2952911872 | bytes 26035200 | tf_op jit(solution)/shard_map/dot_general | solution.py:21
  165.2 0.0 copy-start.1
  165.2 1.6 copy-done.1
  166.8 0.0 copy-done.3
  166.8 2.8 fusion.31
  169.6 47.5 %psum.28 = f32[150,32]{0,1:T(8,128)S(1)} all-reduce(f32[150,32]{0,1:T(8,128)S(1)} %fusion.31), channel_id=1, replica_groups=mesh['replica'=16,'mp'=16] {'replica'}, use_global_device_ids=true, to_apply=%region_0.0 | all-reduce | flops 4800 | bytes 38400 | tf_op jit(solution)/shard_map/psum | solution.py:25
  217.1 0.2 fusion.18
  217.3 67.4 %psum.29 = f32[32,32]{0,1:T(8,128)S(1)} all-reduce(f32[32,32]{0,1:T(8,128)S(1)} %fusion.18), channel_id=1, replica_groups=mesh['replica'=16,'mp'=16] {'mp'}, use_global_device_ids=true, to_apply=%region_1.0 | all-reduce | flops 1024 | bytes 8192 | tf_op jit(solution)/shard_map/psum | solution.py:26
  284.6 0.1 copy.9
  284.7 2.9 cholesky.16
  287.6 0.6 compare_reduce_fusion
  288.3 0.7 fusion.20
  288.9 2.4 custom-call.7
  291.4 0.2 fusion.16
  291.6 4.7 fusion.32
  296.3 0.0 copy-start.4
  296.3 0.0 all-reduce.3.cloned.1.call-update
  296.3 0.2 all-reduce.5.cloned.1.call-start
  296.6 109.7 %all-reduce.3.cloned.1.call-done = f32[4800,32]{0,1:T(8,128)} async-done(((f32[4800,32]{0,1:T(8,128)}), f32[4800,32]{0,1:T(8,128)}) %all-reduce.3.cloned.1.call-update) | async-done | bytes 614416 | tf_op jit(solution)/shard_map/psum | solution.py:30
  406.3 0.0 all-reduce.5.cloned.1.call-update
  406.3 0.0 copy-done
  406.4 0.0 copy-done.4
  406.4 11.3 %fusion.4 = bf16[150,2048]{1,0:T(8,128)(2,1)} fusion(bf16[150,2048]{1,0:T(8,128)(2,1)S(1)} %copy-done.4, bf16[150,4800]{1,0:T(8,128)(2,1)S(1)} %copy-done, bf16[2048,4800]{0,1:T(8,128)(2,1)} %all-gather.2.cloned.1.call-done), kind=kOutput, calls=%fused_computation.11 | convolution fusion | flops 2955571200 | bytes 22329600 | tf_op jit(solution)/shard_map/kf,hf->hk/dot_general | solution.py:17
  417.7 87.6 %all-reduce.5.cloned.1.call-done = f32[4800,32]{0,1:T(8,128)} async-done(((f32[4800,32]{0,1:T(8,128)}), f32[4800,32]{0,1:T(8,128)}) %all-reduce.5.cloned.1.call-update) | async-done | bytes 614416 | tf_op jit(solution)/shard_map/psum | solution.py:30
  505.2 1.1 broadcast_multiply_fusion
  506.4 0.0 copy-start.2
  506.4 4.6 fusion
  511.0 0.0 copy-done.2
  511.0 4.6 copy.10
  (2 shorter events, 0.0 us)
Async XLA Ops:
  7.2 399.2 %copy-start = (bf16[150,4800]{1,0:T(8,128)(2,1)S(1)}, bf16[150,4800]{1,0:T(8,128)(2,1)}, u32[]{:S(2)}) copy-start(bf16[150,4800]{1,0:T(8,128)(2,1)} %param.7) | copy-start | bytes 4320004
  7.2 146.7 %all-gather.2.cloned.1.call-start = ((), (), s32[]{:S(2)}) async-start(), calls=%async_computation | async-start | bytes 20889600 | tf_op jit(solution)/shard_map/all_gather | solution.py:16
  7.9 158.9 %copy-start.3 = (f32[4800,32]{0,1:T(8,128)S(1)}, f32[4800,32]{0,1:T(8,128)}, u32[]{:S(2)}) copy-start(f32[4800,32]{0,1:T(8,128)} %param.9) | copy-start | bytes 1843204
  7.9 398.4 %all-reduce.3.cloned.1.call-start = ((), (), s32[]{:S(2)}) async-start(), calls=%async_computation.1 | async-start | bytes 1245184 | tf_op jit(solution)/shard_map/psum | solution.py:30
  165.2 1.7 copy-start.1
  296.3 110.0 %copy-start.4 = (bf16[150,2048]{1,0:T(8,128)(2,1)S(1)}, bf16[150,2048]{1,0:T(8,128)(2,1)}, u32[]{:S(2)}) copy-start(bf16[150,2048]{1,0:T(8,128)(2,1)} %param.5) | copy-start | bytes 1843204
  296.3 208.9 %all-reduce.5.cloned.1.call-start = ((), (), s32[]{:S(2)}) async-start(), calls=%async_computation.2 | async-start | bytes 1245184 | tf_op jit(solution)/shard_map/psum | solution.py:30
  506.4 4.6 copy-start.2
Sparse Core Ops, SparseCore 0:
  10.4 143.3 all-gather.1
  296.5 109.8 all-reduce.2
  410.0 95.2 all-reduce.4
